TPU v7x, 32 devices: a whole 2x2x4 slice. The times are simulated.
32 devices in a mesh: pair: 16 (over z, y, x), vir: 2 (over core).
Axes of the slice: x: 2, y: 2, z: 4, core: 2. Of those that a mesh axis runs over, the one named last changes fastest.
Arguments:
- amplitudes: bfloat16 [40960, 1024], P('pair', 'vir'), may hold values from -6 to 6
- cycle_ints: bfloat16 [40960, 1024], P('pair', 'vir'), may hold values from -6 to 6
- int_rows: bfloat16 [1024, 1024], P('pair', 'vir'), may hold values from -6 to 6
- row_dest: int32 [1024, 2], P('pair'), may hold values from 0 to 15, all different within a row; in each aligned block of 64 rows (0 to 63, 64 to 127, ...) at most 16 rows name the same one
- vir_energy: float32 [1024], P('vir'), may hold values from 0.5 to 4
- occ_energy: float32 [40960], P('pair'), may hold values from -2 to -0.2
Outputs:
- residual: bfloat16 [40960, 1024], P('pair', 'vir')
Inputs may be any that keep to these rules, and one draw needn't show every extreme that they name: `row_dest`: each integral row names 2 different pair groups; among the 64 rows of one pair group no group is named more than 16 times, a bound that some block reaches.
All inputs are finite; a program needn't handle non-finite values.
Results may differ from a plain program's by a relative error of at most 0.008.
Values may be sent and summed in bfloat16 or wider, within the bound.
A program may use at most 64 MiB of HBM per device.

v0:
```python
import math

import jax
import jax.numpy as jnp
from jax import lax
from jax.sharding import PartitionSpec as P

SLOTS = 256


def dispatch(int_rows, row_dest, groups, capacity):
    rows = int_rows.shape[0]
    group = jnp.arange(groups, dtype=jnp.int32)
    member = jnp.any(row_dest[None, :, :] == group[:, None, None], axis=2)
    before = jnp.arange(rows)[:, None] < jnp.arange(rows)[None, :]
    rank = jnp.dot(
        member.astype(jnp.bfloat16), before.astype(jnp.bfloat16), preferred_element_type=jnp.float32
    ).astype(jnp.int32)
    slot = jnp.arange(capacity, dtype=jnp.int32)
    select = member[:, None, :] & (rank[:, None, :] == slot[None, :, None])
    select = select.reshape(groups * capacity, rows).astype(int_rows.dtype)
    return jnp.dot(select, int_rows, preferred_element_type=jnp.float32).astype(int_rows.dtype)


def body(amplitudes, cycle_ints, int_rows, row_dest, vir_energy, occ_energy):
    groups = lax.axis_size("pair")
    row_count, local_width = amplitudes.shape
    full_width = local_width * lax.axis_size("vir")
    capacity = SLOTS // groups
    gathered = lax.all_gather(amplitudes, "vir", axis=1, tiled=True)
    cross_part = lax.dot_general(
        gathered, cycle_ints, (((0,), (0,)), ((), ())), preferred_element_type=jnp.float32
    )
    scale_cycle = math.sqrt(row_count * groups * full_width)
    cross_half = lax.psum((cross_part / scale_cycle).astype(jnp.bfloat16), "pair")
    outgoing = dispatch(int_rows, row_dest, groups, capacity)
    arrived = lax.all_to_all(
        outgoing.reshape(groups, capacity, local_width),
        "pair",
        split_axis=0,
        concat_axis=0,
        tiled=True,
    ).reshape(groups * capacity, local_width)
    chosen = lax.all_gather(arrived, "vir", axis=1, tiled=True)
    coefficient = lax.dot_general(
        gathered, chosen, (((1,), (1,)), ((), ())), preferred_element_type=jnp.float32
    ) / math.sqrt(full_width)
    ladder = jnp.dot(
        coefficient.astype(jnp.bfloat16), arrived, preferred_element_type=jnp.float32
    ) / math.sqrt(SLOTS)
    energy = (vir_energy[None, :] - occ_energy[:, None]) * amplitudes.astype(jnp.float32)
    cycle_term = jnp.dot(gathered, cross_half, preferred_element_type=jnp.float32)
    return (cycle_term + ladder + energy).astype(jnp.bfloat16)


def solution(mesh):
    return jax.shard_map(
        body,
        mesh=mesh,
        in_specs=(
            P("pair", "vir"),
            P("pair", "vir"),
            P("pair", "vir"),
            P("pair", None),
            P("vir"),
            P("pair"),
        ),
        out_specs=P("pair", "vir"),
        check_vma=False,
    )
```

profile of v0, /device:TPU:0, one launch (start us, length us, event | category | flops | bytes accessed | tf_op | source)
XLA Modules:
  0.0 178.0 jit_solution(11613272002490482271)
XLA Ops:
  6.5 0.0 copy-start
  6.5 0.0 all-gather.2.cloned.1.call-start
  6.5 0.7 all-gather.2.cloned.1.call-update
  7.3 0.0 all-reduce.2.cloned.1.call-start
  7.3 0.1 eq.39
  7.4 0.7 fusion.4
  8.1 0.0 copy-start.1
  8.1 18.8 %all-gather.2.cloned.1.call-done = bf16[2560,1024]{1,0:T(8,128)(2,1)} async-done(((bf16[2560,512]{1,0:T(8,128)(2,1)}), bf16[2560,1024]{1,0:T(8,128)(2,1)}) %all-gather.2.cloned.1.call-update) | async-done | bytes 5242896 | tf_op jit(solution)/shard_map/all_gather | solution.py:30
  26.9 0.0 copy-done
  26.9 6.4 %multiply_convert_fusion = bf16[1024,512]{1,0:T(8,128)(2,1)} fusion(bf16[2560,1024]{1,0:T(8,128)(2,1)} %all-gather.2.cloned.1.call-done, bf16[2560,512]{1,0:T(8,128)(2,1)S(1)} %copy-done), kind=kOutput, calls=%fused_computation.5 | convolution fusion | flops 2685403136 | bytes 8912896 | tf_op jit(solution)/shard_map/dot_general | solution.py:31
  33.3 0.0 all-reduce.2.cloned.1.call-update
  33.3 0.1 convolution_convert_fusion.1
  33.4 0.1 fusion.3
  33.5 0.0 copy-done.1
  33.5 0.9 convolution_convert_fusion
  34.4 6.8 %all-to-all-start = ((bf16[16,16,512]{2,1,0:T(8,128)(2,1)}), bf16[16,16,512]{2,1,0:T(8,128)(2,1)S(1)}, u32[]{:S(2)}, u32[]{:S(2)}) async-start(bf16[16,16,512]{2,1,0:T(8,128)(2,1)} %bitcast.3), calls=%async_computation | async-start | bytes 524288 | tf_op jit(solution)/shard_map/all_to_all | solution.py:37
  41.2 4.4 %copy.12 = bf16[2560,512]{0,1:T(8,128)(2,1)} copy(bf16[2560,512]{1,0:T(8,128)(2,1)} %param.6) | data formatting | bytes 5242880 | tf_op args[0]
  45.6 9.9 %all-to-all-done = bf16[16,16,512]{2,1,0:T(8,128)(2,1)S(1)} async-done(((bf16[16,16,512]{2,1,0:T(8,128)(2,1)}), bf16[16,16,512]{2,1,0:T(8,128)(2,1)S(1)}, u32[]{:S(2)}, u32[]{:S(2)}) %all-to-all-start) | async-done | bytes 262176 | tf_op jit(solution)/shard_map/all_to_all | solution.py:37
  55.5 2.2 %all_gather.7 = bf16[256,1024]{1,0:T(8,128)(2,1)S(1)} all-gather(bf16[256,512]{1,0:T(8,128)(2,1)S(1)} %bitcast.24), channel_id=1, replica_groups=mesh['pair'=16,'vir'=2] {'vir'}, dimensions={1}, use_global_device_ids=true | all-gather | bytes 786432 | tf_op jit(solution)/shard_map/all_gather | solution.py:44
  57.7 0.0 copy-start.2
  57.7 0.0 copy-start.3
  57.7 92.0 %all-reduce.2.cloned.1.call-done = bf16[1024,512]{1,0:T(8,128)(2,1)} async-done(((bf16[1024,512]{1,0:T(8,128)(2,1)}), bf16[1024,512]{1,0:T(8,128)(2,1)}) %all-reduce.2.cloned.1.call-update) | async-done | bytes 1048592 | tf_op jit(solution)/shard_map/psum | solution.py:35
  149.7 8.1 %fusion.6 = f32[512,2560]{1,0:T(8,128)} fusion(bf16[1024,512]{1,0:T(8,128)(2,1)} %all-reduce.2.cloned.1.call-done, bf16[2560,1024]{1,0:T(8,128)(2,1)} %all-gather.2.cloned.1.call-done), kind=kOutput, calls=%fused_computation.14 | convolution fusion | flops 2684354560 | bytes 11534336 | tf_op jit(solution)/shard_map/dot_general | solution.py:52
  157.8 0.0 copy-done.2
  157.8 0.0 copy-done.3
  157.8 9.0 %fusion.1 = bf16[2560,512]{0,1:T(8,128)(2,1)} fusion(f32[512,2560]{1,0:T(8,128)} %fusion.6, bf16[2560,512]{0,1:T(8,128)(2,1)} %copy.12, bf16[256,512]{1,0:T(8,128)(2,1)S(1)} %bitcast.25, f32[2560]{0:T(1024)S(1)} %copy-done.2, f32[512]{0:T(512)S(1)} %copy-done.3, bf16[256,1024]{1,0:T(8,128)(2,1)S(1)} %all_gather.7, ...), kind=kOutput, calls=%fused_computation.2 | convolution fusion | flops 2023751680 | bytes 16527360 | tf_op jit(solution)/shard_map/dot_general | solution.py:48
  166.8 4.4 %copy.13 = bf16[2560,512]{1,0:T(8,128)(2,1)} copy(bf16[2560,512]{0,1:T(8,128)(2,1)} %fusion.1) | data formatting | bytes 5242880 | tf_op jit(solution)/shard_map/convert_element_type | solution.py:53
  (1 shorter events, 0.0 us)
Async XLA Ops:
  6.5 20.3 %copy-start = (bf16[2560,512]{1,0:T(8,128)(2,1)S(1)}, bf16[2560,512]{1,0:T(8,128)(2,1)}, u32[]{:S(2)}) copy-start(bf16[2560,512]{1,0:T(8,128)(2,1)} %param.7) | copy-start | bytes 7864324
  6.5 20.3 %all-gather.2.cloned.1.call-start = ((), (), s32[]{:S(2)}) async-start(), calls=%async_computation.1 | async-start | bytes 7864320 | tf_op jit(solution)/shard_map/all_gather | solution.py:30
  7.3 142.4 %all-reduce.2.cloned.1.call-start = ((), (), s32[]{:S(2)}) async-start(), calls=%async_computation.2 | async-start | bytes 2097152 | tf_op jit(solution)/shard_map/psum | solution.py:35
  8.1 25.4 %copy-start.1 = (bf16[64,512]{1,0:T(8,128)(2,1)S(1)}, bf16[64,512]{1,0:T(8,128)(2,1)}, u32[]{:S(2)}) copy-start(bf16[64,512]{1,0:T(8,128)(2,1)} %param.8) | copy-start | bytes 196612
  34.4 21.1 %all-to-all-start = ((bf16[16,16,512]{2,1,0:T(8,128)(2,1)}), bf16[16,16,512]{2,1,0:T(8,128)(2,1)S(1)}, u32[]{:S(2)}, u32[]{:S(2)}) async-start(bf16[16,16,512]{2,1,0:T(8,128)(2,1)} %bitcast.3), calls=%async_computation | async-start | bytes 524288 | tf_op jit(solution)/shard_map/all_to_all | solution.py:37
  57.7 100.1 %copy-start.2 = (f32[2560]{0:T(1024)S(1)}, f32[2560]{0:T(1024)}, u32[]{:S(2)}) copy-start(f32[2560]{0:T(1024)} %param.11) | copy-start | bytes 30724
  57.7 100.1 %copy-start.3 = (f32[512]{0:T(512)S(1)}, f32[512]{0:T(512)}, u32[]{:S(2)}) copy-start(f32[512]{0:T(512)} %param.10) | copy-start | bytes 6148
Sparse Core Ops, SparseCore 0:
  8.9 17.9 all-gather.1
  33.4 116.2 all-reduce.1
where the time goes:
time: 178 us
  waiting for transfers between devices  121 us (68%)
  matrix products  24.5 us (14%)
  between operations  13.4 us (8%)
  local copies, waits for them, and re-layouts  8.86 us (5%)
  starting transfers between devices  6.82 us (4%)
  blocking collectives  2.17 us (1%)
    psum x1, waiting for transfers between devices, body(): lax.psum((cross_part / scale_cycle).astype(jnp.bfloat16), 'pair')  92 us
    all_gather x1, waiting for transfers between devices, body(): gathered = lax.all_gather(amplitudes, 'vir', axis=1, tiled=True)  18.8 us
    all_to_all x1, waiting for transfers between devices, body(): lax.all_to_all(outgoing.reshape(groups, capacity, local_width), 'pair', s...  9.9 us
    dot_general x1, matrix products, body(): jnp.dot(coefficient.astype(jnp.bfloat16), arrived, preferred_element_type...  9.01 us
    dot_general x1, matrix products, body(): jnp.dot(gathered, cross_half, preferred_element_type=jnp.float32)  8.08 us
    all_to_all x1, starting transfers between devices, body(): lax.all_to_all(outgoing.reshape(groups, capacity, local_width), 'pair', s...  6.78 us
    dot_general x1, matrix products, body(): lax.dot_general(gathered, cycle_ints, (((0,), (0,)), ((), ())), preferred...  6.4 us
    unnamed x9, local copies, waits for them, and re-layouts  4.4 us
  transfers between devices with their start and end apart: 3, of which 3 were waited for; matrix products, arithmetic and copies ran while one was open for 4% of the time, Pallas kernels for 0%

commit v1 on v0

--- a/solution.py
+++ b/solution.py
@@ -3,6 +3,8 @@
 import jax
 import jax.numpy as jnp
 from jax import lax
+from jax.experimental import pallas as pl
+from jax.experimental.pallas import tpu as pltpu
 from jax.sharding import PartitionSpec as P
 
 SLOTS = 256
@@ -53,9 +55,251 @@
     return (cycle_term + ladder + energy).astype(jnp.bfloat16)
 
 
+DEPTH, PLANE, HALVES, PIECES = 4, 4, 2, 4
+F32, BF16 = jnp.float32, jnp.bfloat16
+
+
+def rows_at(start, size):
+    return pl.ds(pl.multiple_of(start, size), size)
+
+
+def kernel(
+    amp, cyc, rows, dest, vir_e, occ_e, out,
+    other, part, plane_in, zsum, z_in, full, outgoing, arr, arr_o, acc,
+    amp_sem, route_sem, arr_sem, plane_sem, z_sem, gz_sem, gp_sem,
+):
+    groups = DEPTH * PLANE
+    me, v = lax.axis_index("pair"), lax.axis_index("vir")
+    z, q = me // PLANE, me % PLANE
+    count, width = amp.shape
+    full_width = 2 * width
+    capacity = SLOTS // groups
+    half = width // HALVES
+    block = full_width // PLANE
+    piece = block // DEPTH
+
+    barrier = pltpu.get_barrier_semaphore()
+    for k in range(1, groups):
+        pl.semaphore_signal(
+            barrier, inc=1, device_id=((me + k) % groups, v), device_id_type=pl.DeviceIdType.MESH
+        )
+    pl.semaphore_signal(barrier, inc=1, device_id=(me, 1 - v), device_id_type=pl.DeviceIdType.MESH)
+
+    def copy(src, dst, sem, index, device):
+        return pltpu.make_async_remote_copy(
+            src_ref=src,
+            dst_ref=dst,
+            send_sem=sem.at[(0, *index)],
+            recv_sem=sem.at[(1, *index)],
+            device_id=device,
+            device_id_type=pl.DeviceIdType.MESH,
+        )
+
+    group = lax.broadcasted_iota(jnp.int32, (SLOTS, rows.shape[0]), 0) // capacity
+    slot = lax.broadcasted_iota(jnp.int32, (SLOTS, rows.shape[0]), 0) % capacity
+    member = group == dest[0:1, :]
+    for k in range(1, dest.shape[0]):
+        member = member | (group == dest[k : k + 1, :])
+    tri = (rows.shape[0], rows.shape[0])
+    before = lax.broadcasted_iota(jnp.int32, tri, 0) < lax.broadcasted_iota(jnp.int32, tri, 1)
+    rank = jnp.dot(
+        jnp.where(member, 1.0, 0.0).astype(BF16),
+        jnp.where(before, 1.0, 0.0).astype(BF16),
+        preferred_element_type=F32,
+    )
+    select = jnp.where(member & (rank == slot.astype(F32)), 1.0, 0.0).astype(BF16)
+    outgoing[...] = jnp.dot(select, rows[...], preferred_element_type=F32).astype(BF16)
+    pl.semaphore_wait(barrier, groups)
+
+    step = count // PIECES
+    amp_copies = [
+        copy(amp.at[pl.ds(i * step, step)], other.at[pl.ds(i * step, step)], amp_sem, (i,), (me, 1 - v))
+        for i in range(PIECES)
+    ]
+    for c in amp_copies:
+        c.start()
+    route_copies = []
+    for k in range(1, groups):
+        to = (me + k) % groups
+        c = copy(
+            outgoing.at[rows_at(to * capacity, capacity)],
+            arr.at[rows_at(me * capacity, capacity)],
+            route_sem, (k - 1,), (to, v),
+        )
+        c.start()
+        route_copies.append(c)
+    mine = rows_at(me * capacity, capacity)
+    arr[mine, :] = outgoing[mine, :]
+
+    plane_copies = [
+        [
+            copy(
+                part.at[h, rows_at((q + d) % PLANE * block, block)],
+                plane_in.at[h, d - 1],
+                plane_sem, (h, d - 1), (z * PLANE + (q + d) % PLANE, v),
+            )
+            for d in range(1, PLANE)
+        ]
+        for h in range(HALVES)
+    ]
+
+    def cross(src, owner, h):
+        for j in range(width // block):
+            value = lax.dot_general(
+                src[:, pl.ds(j * block, block)],
+                cyc[:, pl.ds(h * half, half)],
+                (((0,), (0,)), ((), ())),
+                preferred_element_type=F32,
+            )
+            part[h, rows_at(owner * width + j * block, block), :] = value.astype(BF16)
+        for d in range(1, PLANE):
+            target = (q + d) % PLANE
+
+            @pl.when(target // (PLANE // 2) == owner)
+            def _():
+                plane_copies[h][d - 1].start()
+
+    for h in range(HALVES):
+        cross(amp, v, h)
+    for c in route_copies:
+        c.wait_recv()
+    arr_copy = copy(arr, arr_o, arr_sem, (0,), (me, 1 - v))
+    arr_copy.start()
+    for c in amp_copies:
+        c.wait_recv()
+    for h in range(HALVES):
+        cross(other, 1 - v, h)
+    arr_copy.wait_recv()
+
+    tile = 256
+    contract = (((1,), (1,)), ((), ()))
+
+    def ladder(t, carry):
+        at = rows_at(t * tile, tile)
+        mine = amp[at, :]
+        value = lax.dot_general(mine, arr[...], contract, preferred_element_type=F32)
+        value += lax.dot_general(other[at, :], arr_o[...], contract, preferred_element_type=F32)
+        value = (value / math.sqrt(full_width)).astype(BF16)
+        value = jnp.dot(value, arr[...], preferred_element_type=F32) / math.sqrt(SLOTS)
+        for s in range(tile // 128):
+            line = jnp.broadcast_to(occ_e[pl.ds(t * (tile // 128) + s, 1), :], (128, 128)).T
+            for b in range(width // 128):
+                cols = slice(b * 128, (b + 1) * 128)
+                sub = slice(s * 128, (s + 1) * 128)
+                acc[pl.ds(pl.multiple_of(t * tile + s * 128, 128), 128), cols] = value[sub, cols] + (
+                    vir_e[:, cols] - line
+                ) * mine[sub, cols].astype(F32)
+        return carry
+
+    tiles = count // tile
+    z_copies, gz_copies, gp_copies = [], [], []
+    for h in range(HALVES):
+        lax.fori_loop(h * tiles // HALVES, (h + 1) * tiles // HALVES, ladder, 0)
+        for c in plane_copies[h]:
+            c.wait_recv()
+        total = part[h, rows_at(q * block, block), :].astype(F32)
+        for d in range(1, PLANE):
+            total += plane_in[h, d - 1].astype(F32)
+        zsum[h] = total.astype(BF16)
+        for e in range(1, DEPTH):
+            to = (z + e) % DEPTH
+            c = copy(
+                zsum.at[h, rows_at(to * piece, piece)],
+                z_in.at[h, e - 1],
+                z_sem, (h, e - 1), (to * PLANE + q, v),
+            )
+            c.start()
+            z_copies.append(c)
+    scale = math.sqrt(count * groups * full_width)
+    own = rows_at((q * DEPTH + z) * piece, piece)
+    for h in range(HALVES):
+        for e in range(1, DEPTH):
+            z_copies[h * (DEPTH - 1) + e - 1].wait_recv()
+        total = zsum[h, rows_at(z * piece, piece), :].astype(F32)
+        for e in range(1, DEPTH):
+            total += z_in[h, e - 1].astype(F32)
+        full[h, own, :] = (total / scale).astype(BF16)
+        for e in range(1, DEPTH):
+            c = copy(
+                full.at[h, own], full.at[h, own], gz_sem, (h, e - 1), ((z + e) % DEPTH * PLANE + q, v)
+            )
+            c.start()
+            gz_copies.append(c)
+    whole = rows_at(q * block, block)
+    for h in range(HALVES):
+        for e in range(1, DEPTH):
+            gz_copies[h * (DEPTH - 1) + e - 1].wait_recv()
+        for d in range(1, PLANE):
+            c = copy(
+                full.at[h, whole], full.at[h, whole],
+                gp_sem, (h, d - 1), (z * PLANE + (q + d) % PLANE, v),
+            )
+            c.start()
+            gp_copies.append(c)
+    for h in range(HALVES):
+        for d in range(1, PLANE):
+            gp_copies[h * (PLANE - 1) + d - 1].wait_recv()
+        cols = slice(h * half, (h + 1) * half)
+
+        def cycle(t, carry):
+            at = rows_at(t * tile, tile)
+            value = jnp.dot(
+                amp[at, :], full[h, rows_at(v * width, width), :], preferred_element_type=F32
+            )
+            value += jnp.dot(
+                other[at, :], full[h, rows_at((1 - v) * width, width), :], preferred_element_type=F32
+            )
+            out[at, cols] = (value + acc[at, cols]).astype(BF16)
+            return carry
+
+        lax.fori_loop(0, tiles, cycle, 0)
+    plane_all = [c for part_of in plane_copies for c in part_of]
+    for c in amp_copies + route_copies + [arr_copy] + plane_all + z_copies + gz_copies + gp_copies:
+        c.wait_send()
+
+
+def fused(amplitudes, cycle_ints, int_rows, row_dest, vir_energy, occ_energy):
+    count, width = amplitudes.shape
+    groups = DEPTH * PLANE
+    half, block = width // HALVES, 2 * width // PLANE
+    dma = pltpu.SemaphoreType.DMA
+    return pl.pallas_call(
+        kernel,
+        out_shape=jax.ShapeDtypeStruct((count, width), BF16),
+        in_specs=[pl.BlockSpec(memory_space=pltpu.VMEM)] * 6,
+        out_specs=pl.BlockSpec(memory_space=pltpu.VMEM),
+        scratch_shapes=[
+            pltpu.VMEM((count, width), BF16),
+            pltpu.VMEM((HALVES, 2 * width, half), BF16),
+            pltpu.VMEM((HALVES, PLANE - 1, block, half), BF16),
+            pltpu.VMEM((HALVES, block, half), BF16),
+            pltpu.VMEM((HALVES, DEPTH - 1, block // DEPTH, half), BF16),
+            pltpu.VMEM((HALVES, 2 * width, half), BF16),
+            pltpu.VMEM((SLOTS, width), BF16),
+            pltpu.VMEM((SLOTS, width), BF16),
+            pltpu.VMEM((SLOTS, width), BF16),
+            pltpu.VMEM((count, width), F32),
+            dma((2, PIECES)),
+            dma((2, groups - 1)),
+            dma((2, 1)),
+            dma((2, HALVES, PLANE - 1)),
+            dma((2, HALVES, DEPTH - 1)),
+            dma((2, HALVES, DEPTH - 1)),
+            dma((2, HALVES, PLANE - 1)),
+        ],
+        compiler_params=pltpu.CompilerParams(
+            collective_id=0, has_side_effects=True, vmem_limit_bytes=48 * 2**20
+        ),
+    )(
+        amplitudes, cycle_ints, int_rows, row_dest.T,
+        vir_energy.reshape(1, width), occ_energy.reshape(count // 128, 128),
+    )
+
+
 def solution(mesh):
+    fits = mesh.shape["pair"] == DEPTH * PLANE and mesh.shape["vir"] == 2
     return jax.shard_map(
-        body,
+        fused if fits else body,
         mesh=mesh,
         in_specs=(
             P("pair", "vir"),

time: 178 us -> 54 us (0.30)
  waiting for transfers between devices: 121 us -> 0 us
  Pallas kernels: 0 us -> 47.5 us
  matrix products: 24.5 us -> 0 us
  between operations: 13.4 us -> 0.01 us
  starting transfers between devices: 6.82 us -> 0 us
  local copies, waits for them, and re-layouts: 8.86 us -> 6.14 us
  blocking collectives: 2.17 us -> 0 us
    psum x1 -> x0, waiting for transfers between devices: 92 us -> none  [body(): lax.psum((cross_part / scale_cycle).astype(jnp.bfloat16), 'pair')]
    pallas_call x0 -> x1, Pallas kernels: none -> 47.5 us  [fused(): pl.pallas_call(kernel, out_shape=jax.ShapeDtypeStruct((count, width), BF1...]
    dot_general x5 -> x0, matrix products: 24.5 us -> none  [the longest x1 9.01 us: body(): jnp.dot(coefficient.astype(jnp.bfloat16), arrived, preferred_element_type...]
    all_gather x1 -> x0, waiting for transfers between devices: 18.8 us -> none  [body(): gathered = lax.all_gather(amplitudes, 'vir', axis=1, tiled=True)]
    all_to_all x1 -> x0, waiting for transfers between devices: 9.9 us -> none  [body(): lax.all_to_all(outgoing.reshape(groups, capacity, local_width), 'pair', s...]
    all_to_all x1 -> x0, starting transfers between devices: 6.78 us -> none  [body(): lax.all_to_all(outgoing.reshape(groups, capacity, local_width), 'pair', s...]
    convert_element_type x1 -> x0, local copies, waits for them, and re-layouts: 4.38 us -> none  [body(): return (cycle_term + ladder + energy).astype(jnp.bfloat16)]
    all_gather x1 -> x0, blocking collectives: 2.17 us -> none  [body(): chosen = lax.all_gather(arrived, 'vir', axis=1, tiled=True)]
  transfers between devices with their start and end apart: 3 -> 0, of which waited for: 3 -> 0; matrix products, arithmetic and copies ran while one was open for 4% -> 0% of each run, Pallas kernels for 0% -> 0%
where the time goes in v1:
time: 54 us; the launch traced here: 53.6 us
  Pallas kernels  47.5 us (88%)
  local copies, waits for them, and re-layouts  6.14 us (11%)
    pallas_call x1, Pallas kernels, fused(): pl.pallas_call(kernel, out_shape=jax.ShapeDtypeStruct((count, width), BF1...  47.5 us
    unnamed x11, local copies, waits for them, and re-layouts  6.14 us

profile of v1, /device:TPU:0, one launch (start us, length us, event | category | flops | bytes accessed | tf_op | source)
XLA Modules:
  0.0 53.6 jit_solution(4928174576049232581)
XLA Ops:
  0.0 0.0 copy-start
  0.0 1.7 %copy-done = bf16[2560,512]{1,0:T(8,128)(2,1)S(1)} copy-done((bf16[2560,512]{1,0:T(8,128)(2,1)S(1)}, bf16[2560,512]{1,0:T(8,128)(2,1)}, u32[]{:S(2)}) %copy-start) | copy-done | bytes 2621464
  1.7 0.0 copy-start.1
  1.7 0.8 %copy-done.1 = bf16[64,512]{1,0:T(8,128)(2,1)S(1)} copy-done((bf16[64,512]{1,0:T(8,128)(2,1)S(1)}, bf16[64,512]{1,0:T(8,128)(2,1)}, u32[]{:S(2)}) %copy-start.1) | copy-done | bytes 65560
  2.6 0.0 copy-start.2
  2.6 0.7 %copy-done.2 = f32[2560]{0:T(1024)S(1)} copy-done((f32[2560]{0:T(1024)S(1)}, f32[2560]{0:T(1024)}, u32[]{:S(2)}) %copy-start.2) | copy-done | bytes 10264
  3.3 0.0 copy-start.3
  3.3 0.7 %copy-done.3 = f32[512]{0:T(512)S(1)} copy-done((f32[512]{0:T(512)S(1)}, f32[512]{0:T(512)}, u32[]{:S(2)}) %copy-start.3) | copy-done | bytes 2072
  4.0 0.0 copy-start.4
  4.0 0.7 %copy-done.4 = s32[64,2]{0,1:T(2,128)S(1)} copy-done((s32[64,2]{0,1:T(2,128)S(1)}, s32[64,2]{0,1:T(2,128)}, u32[]{:S(2)}) %copy-start.4) | copy-done | bytes 536
  4.7 47.5 %shard_map.64 = bf16[2560,512]{1,0:T(8,128)(2,1)S(1)} custom-call(bf16[2560,512]{1,0:T(8,128)(2,1)S(1)} %copy-done, bf16[2560,512]{1,0:T(8,128)(2,1)} %cyc.1, bf16[64,512]{1,0:T(8,128)(2,1)S(1)} %copy-done.1, s32[2,64]{1,0:T(2,128)S(1)} %bitcast.5, f32[1,512]{1,0:T(1,128)S(1)} %bitcast.4, f32[20,128]{1,0:T(8,128)S(1)} %bitcast.3), custom_call_target="tpu_custom_call" | custom-call | tf_op jit(solution)/shard_map/pallas_call | solution.py:266
  52.2 1.5 %copy.8 = bf16[2560,512]{1,0:T(8,128)(2,1)} copy(bf16[2560,512]{1,0:T(8,128)(2,1)S(1)} %shard_map.64) | data formatting | bytes 5242880
Async XLA Ops:
  0.0 1.7 %copy-start = (bf16[2560,512]{1,0:T(8,128)(2,1)S(1)}, bf16[2560,512]{1,0:T(8,128)(2,1)}, u32[]{:S(2)}) copy-start(bf16[2560,512]{1,0:T(8,128)(2,1)} %amp.1) | copy-start | bytes 7864324
  1.7 0.8 %copy-start.1 = (bf16[64,512]{1,0:T(8,128)(2,1)S(1)}, bf16[64,512]{1,0:T(8,128)(2,1)}, u32[]{:S(2)}) copy-start(bf16[64,512]{1,0:T(8,128)(2,1)} %rows.1) | copy-start | bytes 196612
  2.6 0.7 %copy-start.2 = (f32[2560]{0:T(1024)S(1)}, f32[2560]{0:T(1024)}, u32[]{:S(2)}) copy-start(f32[2560]{0:T(1024)} %param.11) | copy-start | bytes 30724
  3.3 0.7 %copy-start.3 = (f32[512]{0:T(512)S(1)}, f32[512]{0:T(512)}, u32[]{:S(2)}) copy-start(f32[512]{0:T(512)} %param.10) | copy-start | bytes 6148
  4.0 0.7 %copy-start.4 = (s32[64,2]{0,1:T(2,128)S(1)}, s32[64,2]{0,1:T(2,128)}, u32[]{:S(2)}) copy-start(s32[64,2]{0,1:T(2,128)} %param.9) | copy-start | bytes 1540

commit v2 on v1

--- a/solution.py
+++ b/solution.py
@@ -64,9 +64,9 @@
 
 
 def kernel(
-    amp, cyc, rows, dest, vir_e, occ_e, out,
-    other, part, plane_in, zsum, z_in, full, outgoing, arr, arr_o, acc,
-    amp_sem, route_sem, arr_sem, plane_sem, z_sem, gz_sem, gp_sem,
+    amp_hbm, cyc_hbm, rows_hbm, dest_hbm, vir_hbm, occ_hbm, out,
+    amp, cyc, rows, dest, vir_e, occ_e, other, part, plane_in, zsum, z_in, full, outgoing, arr, arr_o, acc,
+    load_sem, amp_sem, route_sem, arr_sem, plane_sem, z_sem, gz_sem, gp_sem,
 ):
     groups = DEPTH * PLANE
     me, v = lax.axis_index("pair"), lax.axis_index("vir")
@@ -78,6 +78,17 @@
     block = full_width // PLANE
     piece = block // DEPTH
 
+    loads = [
+        pltpu.make_async_copy(src, dst, load_sem.at[i])
+        for i, (src, dst) in enumerate(
+            (
+                (dest_hbm, dest), (rows_hbm, rows), (vir_hbm, vir_e), (occ_hbm, occ_e),
+                (amp_hbm, amp), (cyc_hbm, cyc),
+            )
+        )
+    ]
+    for c in loads:
+        c.start()
     barrier = pltpu.get_barrier_semaphore()
     for k in range(1, groups):
         pl.semaphore_signal(
@@ -95,6 +106,8 @@
             device_id_type=pl.DeviceIdType.MESH,
         )
 
+    loads[0].wait()
+    loads[1].wait()
     group = lax.broadcasted_iota(jnp.int32, (SLOTS, rows.shape[0]), 0) // capacity
     slot = lax.broadcasted_iota(jnp.int32, (SLOTS, rows.shape[0]), 0) % capacity
     member = group == dest[0:1, :]
@@ -113,7 +126,7 @@
 
     step = count // PIECES
     amp_copies = [
-        copy(amp.at[pl.ds(i * step, step)], other.at[pl.ds(i * step, step)], amp_sem, (i,), (me, 1 - v))
+        copy(amp_hbm.at[pl.ds(i * step, step)], other.at[pl.ds(i * step, step)], amp_sem, (i,), (me, 1 - v))
         for i in range(PIECES)
     ]
     for c in amp_copies:
@@ -159,18 +172,19 @@
             def _():
                 plane_copies[h][d - 1].start()
 
+    for c in loads[2:]:
+        c.wait()
     for h in range(HALVES):
         cross(amp, v, h)
-    for c in route_copies:
+    for c in amp_copies:
         c.wait_recv()
     arr_copy = copy(arr, arr_o, arr_sem, (0,), (me, 1 - v))
-    arr_copy.start()
-    for c in amp_copies:
-        c.wait_recv()
     for h in range(HALVES):
         cross(other, 1 - v, h)
-    arr_copy.wait_recv()
-
+        if h == 0:
+            for c in route_copies:
+                c.wait_recv()
+            arr_copy.start()
     tile = 256
     contract = (((1,), (1,)), ((), ()))
 
@@ -193,8 +207,13 @@
 
     tiles = count // tile
     z_copies, gz_copies, gp_copies = [], [], []
-    for h in range(HALVES):
-        lax.fori_loop(h * tiles // HALVES, (h + 1) * tiles // HALVES, ladder, 0)
+    gp_h = [[] for _ in range(HALVES)]
+    shares = 3 * HALVES - 1
+
+    def some_ladder(i):
+        lax.fori_loop(i * tiles // shares, (i + 1) * tiles // shares, ladder, 0)
+
+    for h in range(HALVES):
         for c in plane_copies[h]:
             c.wait_recv()
         total = part[h, rows_at(q * block, block), :].astype(F32)
@@ -210,6 +229,20 @@
             )
             c.start()
             z_copies.append(c)
+        if h == 0:
+            arr_copy.wait_recv()
+        some_ladder(h)
+    def spread(h, e):
+        at = rows_at((q * DEPTH + (z - e + DEPTH) % DEPTH) * piece, piece)
+        for d in range(1, PLANE):
+            c = copy(
+                full.at[h, at], full.at[h, at],
+                gp_sem, (h, e, d - 1), (z * PLANE + (q + d) % PLANE, v),
+            )
+            c.start()
+            gp_copies.append(c)
+            gp_h[h].append(c)
+
     scale = math.sqrt(count * groups * full_width)
     own = rows_at((q * DEPTH + z) * piece, piece)
     for h in range(HALVES):
@@ -225,20 +258,17 @@
             )
             c.start()
             gz_copies.append(c)
-    whole = rows_at(q * block, block)
+        spread(h, 0)
+        some_ladder(HALVES + h)
     for h in range(HALVES):
         for e in range(1, DEPTH):
             gz_copies[h * (DEPTH - 1) + e - 1].wait_recv()
-        for d in range(1, PLANE):
-            c = copy(
-                full.at[h, whole], full.at[h, whole],
-                gp_sem, (h, d - 1), (z * PLANE + (q + d) % PLANE, v),
-            )
-            c.start()
-            gp_copies.append(c)
-    for h in range(HALVES):
-        for d in range(1, PLANE):
-            gp_copies[h * (PLANE - 1) + d - 1].wait_recv()
+            spread(h, e)
+        if h < HALVES - 1:
+            some_ladder(2 * HALVES + h)
+    for h in range(HALVES):
+        for c in gp_h[h]:
+            c.wait_recv()
         cols = slice(h * half, (h + 1) * half)
 
         def cycle(t, carry):
@@ -266,9 +296,15 @@
     return pl.pallas_call(
         kernel,
         out_shape=jax.ShapeDtypeStruct((count, width), BF16),
-        in_specs=[pl.BlockSpec(memory_space=pltpu.VMEM)] * 6,
+        in_specs=[pl.BlockSpec(memory_space=pl.ANY)] * 6,
         out_specs=pl.BlockSpec(memory_space=pltpu.VMEM),
         scratch_shapes=[
+            pltpu.VMEM((count, width), BF16),
+            pltpu.VMEM((count, width), BF16),
+            pltpu.VMEM(int_rows.shape, BF16),
+            pltpu.VMEM(row_dest.shape[::-1], jnp.int32),
+            pltpu.VMEM((1, width), F32),
+            pltpu.VMEM((count // 128, 128), F32),
             pltpu.VMEM((count, width), BF16),
             pltpu.VMEM((HALVES, 2 * width, half), BF16),
             pltpu.VMEM((HALVES, PLANE - 1, block, half), BF16),
@@ -279,16 +315,17 @@
             pltpu.VMEM((SLOTS, width), BF16),
             pltpu.VMEM((SLOTS, width), BF16),
             pltpu.VMEM((count, width), F32),
+            dma((6,)),
             dma((2, PIECES)),
             dma((2, groups - 1)),
             dma((2, 1)),
             dma((2, HALVES, PLANE - 1)),
             dma((2, HALVES, DEPTH - 1)),
             dma((2, HALVES, DEPTH - 1)),
-            dma((2, HALVES, PLANE - 1)),
+            dma((2, HALVES, DEPTH, PLANE - 1)),
         ],
         compiler_params=pltpu.CompilerParams(
-            collective_id=0, has_side_effects=True, vmem_limit_bytes=48 * 2**20
+            collective_id=0, has_side_effects=True, vmem_limit_bytes=60 * 2**20
         ),
     )(
         amplitudes, cycle_ints, int_rows, row_dest.T,

time: 54 us -> 47.3 us (0.88)
  Pallas kernels: 47.5 us -> 43.7 us
  local copies, waits for them, and re-layouts: 6.14 us -> 3.4 us
    pallas_call x1, Pallas kernels: 47.5 us -> 43.7 us  [fused(): pl.pallas_call(kernel, out_shape=jax.ShapeDtypeStruct((count, width), BF1...]
    unnamed x11 -> x1, local copies, waits for them, and re-layouts: 6.14 us -> 3.4 us
where the time goes in v2:
time: 47.3 us; the launch traced here: 47.1 us
  Pallas kernels  43.7 us (92%)
  local copies, waits for them, and re-layouts  3.4 us (7%)
    pallas_call x1, Pallas kernels, fused(): pl.pallas_call(kernel, out_shape=jax.ShapeDtypeStruct((count, width), BF1...  43.7 us
    unnamed x1, local copies, waits for them, and re-layouts  3.4 us

profile of v2, /device:TPU:0, one launch (start us, length us, event | category | flops | bytes accessed | tf_op | source)
XLA Modules:
  0.0 47.1 jit_solution(17990808153484961029)
XLA Ops:
  0.0 43.7 %shard_map.64 = bf16[2560,512]{1,0:T(8,128)(2,1)} custom-call(bf16[2560,512]{1,0:T(8,128)(2,1)} %amp_hbm.1, bf16[2560,512]{1,0:T(8,128)(2,1)} %cyc_hbm.1, bf16[64,512]{1,0:T(8,128)(2,1)} %rows_hbm.1, s32[2,64]{1,0:T(2,128)} %bitcast.5, f32[1,512]{1,0:T(1,128)} %bitcast.4, f32[20,128]{1,0:T(8,128)} %bitcast.3), custom_call_target="tpu_custom_call" | custom-call | tf_op jit(solution)/shard_map/pallas_call | solution.py:296
  43.7 3.4 %copy.8 = bf16[2560,512]{1,0:T(8,128)(2,1)} copy(bf16[2560,512]{1,0:T(8,128)(2,1)} %shard_map.64) | data formatting | bytes 5242880

commit v3 on v2

--- a/solution.py
+++ b/solution.py
@@ -146,11 +146,14 @@
 
     plane_copies = [
         [
-            copy(
-                part.at[h, rows_at((q + d) % PLANE * block, block)],
-                plane_in.at[h, d - 1],
-                plane_sem, (h, d - 1), (z * PLANE + (q + d) % PLANE, v),
-            )
+            [
+                copy(
+                    part.at[h, rows_at(((q + d) % PLANE * DEPTH + (z + e) % DEPTH) * piece, piece)],
+                    plane_in.at[h, d - 1, rows_at((z + e) % DEPTH * piece, piece)],
+                    plane_sem, (h, e % DEPTH, d - 1), (z * PLANE + (q + d) % PLANE, v),
+                )
+                for e in range(1, DEPTH + 1)
+            ]
             for d in range(1, PLANE)
         ]
         for h in range(HALVES)
@@ -170,7 +173,8 @@
 
             @pl.when(target // (PLANE // 2) == owner)
             def _():
-                plane_copies[h][d - 1].start()
+                for c in plane_copies[h][d - 1]:
+                    c.start()
 
     for c in loads[2:]:
         c.wait()
@@ -214,21 +218,21 @@
         lax.fori_loop(i * tiles // shares, (i + 1) * tiles // shares, ladder, 0)
 
     for h in range(HALVES):
-        for c in plane_copies[h]:
-            c.wait_recv()
-        total = part[h, rows_at(q * block, block), :].astype(F32)
-        for d in range(1, PLANE):
-            total += plane_in[h, d - 1].astype(F32)
-        zsum[h] = total.astype(BF16)
-        for e in range(1, DEPTH):
+        for e in range(1, DEPTH + 1):
             to = (z + e) % DEPTH
-            c = copy(
-                zsum.at[h, rows_at(to * piece, piece)],
-                z_in.at[h, e - 1],
-                z_sem, (h, e - 1), (to * PLANE + q, v),
-            )
-            c.start()
-            z_copies.append(c)
+            for d in range(1, PLANE):
+                plane_copies[h][d - 1][e - 1].wait_recv()
+            at = rows_at(to * piece, piece)
+            total = part[h, rows_at((q * DEPTH + to) * piece, piece), :].astype(F32)
+            for d in range(1, PLANE):
+                total += plane_in[h, d - 1, at, :].astype(F32)
+            zsum[h, at, :] = total.astype(BF16)
+            if e < DEPTH:
+                c = copy(
+                    zsum.at[h, at], z_in.at[h, e - 1], z_sem, (h, e - 1), (to * PLANE + q, v)
+                )
+                c.start()
+                z_copies.append(c)
         if h == 0:
             arr_copy.wait_recv()
         some_ladder(h)
@@ -283,7 +287,7 @@
             return carry
 
         lax.fori_loop(0, tiles, cycle, 0)
-    plane_all = [c for part_of in plane_copies for c in part_of]
+    plane_all = [c for of_half in plane_copies for of_peer in of_half for c in of_peer]
     for c in amp_copies + route_copies + [arr_copy] + plane_all + z_copies + gz_copies + gp_copies:
         c.wait_send()
 
@@ -319,7 +323,7 @@
             dma((2, PIECES)),
             dma((2, groups - 1)),
             dma((2, 1)),
-            dma((2, HALVES, PLANE - 1)),
+            dma((2, HALVES, DEPTH, PLANE - 1)),
             dma((2, HALVES, DEPTH - 1)),
             dma((2, HALVES, DEPTH - 1)),
             dma((2, HALVES, DEPTH, PLANE - 1)),

time: 47.3 us -> 46.9 us (level)
  no operation moved by 1% of the time
where the time goes in v3:
time: 46.9 us; the launch traced here: 46.8 us
  Pallas kernels  43.4 us (93%)
  local copies, waits for them, and re-layouts  3.4 us (7%)
    pallas_call x1, Pallas kernels, fused(): pl.pallas_call(kernel, out_shape=jax.ShapeDtypeStruct((count, width), BF1...  43.4 us
    unnamed x1, local copies, waits for them, and re-layouts  3.4 us

profile of v3, /device:TPU:0, one launch (start us, length us, event | category | flops | bytes accessed | tf_op | source)
XLA Modules:
  0.0 46.8 jit_solution(399994635584908994)
XLA Ops:
  0.0 43.4 %shard_map.64 = bf16[2560,512]{1,0:T(8,128)(2,1)} custom-call(bf16[2560,512]{1,0:T(8,128)(2,1)} %amp_hbm.1, bf16[2560,512]{1,0:T(8,128)(2,1)} %cyc_hbm.1, bf16[64,512]{1,0:T(8,128)(2,1)} %rows_hbm.1, s32[2,64]{1,0:T(2,128)} %bitcast.5, f32[1,512]{1,0:T(1,128)} %bitcast.4, f32[20,128]{1,0:T(8,128)} %bitcast.3), custom_call_target="tpu_custom_call" | custom-call | tf_op jit(solution)/shard_map/pallas_call | solution.py:300
  43.4 3.4 %copy.8 = bf16[2560,512]{1,0:T(8,128)(2,1)} copy(bf16[2560,512]{1,0:T(8,128)(2,1)} %shard_map.64) | data formatting | bytes 5242880
